TPU v7x, 512 devices: a whole 4x4x16 slice. The times are simulated.
512 devices in a mesh: seq: 64 (over x, z), exp: 8 (over y, core).
Axes of the slice: x: 4, y: 4, z: 16, core: 2. Of those that a mesh axis runs over, the one named last changes fastest.
Arguments:
- queries: bfloat16 [4096, 6144], P('seq', 'exp'), may hold values from -6 to 6
- keys: bfloat16 [4096, 6144], P('seq', 'exp'), may hold values from -6 to 6
- values: bfloat16 [4096, 6144], P('seq', 'exp'), may hold values from -6 to 6
- log_decay: float32 [48, 4096], P('exp', 'seq'), may hold values from -1 to 0
- state_in: float32 [48, 128, 128], P('exp'), may hold values from -24 to 24
- norm_gain: float32 [6144], replicated, may hold values from 0.1 to 1.9
- routes: int32 [4096, 2], P('seq'), may hold values from 0 to 7, all different within a row; in each aligned block of 64 rows (0 to 63, 64 to 127, ...) at most 20 rows name the same one
- w_gate: bfloat16 [8, 9216, 6144], P('exp', 'seq'), may hold values from -0.078125 to 0.078125
- w_up: bfloat16 [8, 9216, 6144], P('exp', 'seq'), may hold values from -0.078125 to 0.078125
Outputs:
- expert_hidden: bfloat16 [8, 9216, 1280], P('exp', 'seq')
- state_out: float32 [48, 128, 128], P('exp', 'seq')
Inputs may be any that keep to these rules, and one draw needn't show every extreme that they name: `routes`: each token names two different experts; in each aligned block of 64 tokens no expert is named by more than 20 tokens, and some blocks reach exactly 20.
All inputs are finite; a program needn't handle non-finite values.
Results may differ from a plain program's by a relative error of at most 0.0071.
Values may be sent and summed in bfloat16 or wider, within the bound.
A program may use at most 128 MiB of HBM per device.

v0:
```python
import math
import jax
import jax.numpy as jnp
from jax import lax
from jax.sharding import PartitionSpec as P

CAP = 20
epsilon = 1e-06


def prefix(part, axis, combine, identity):
    place = lax.axis_index(axis)
    gathered = jax.tree.map(lambda a: lax.all_gather(a, axis), part)
    state = jax.tree.map(lambda a, e: jnp.zeros_like(a) + jnp.asarray(e, a.dtype), part, identity)

    def one(hop, state):
        return combine(
            state, jax.tree.map(lambda a: lax.dynamic_index_in_dim(a, hop, 0, False), gathered)
        )

    return lax.fori_loop(0, place, one, state)


def compose(earlier, later_pair):
    return (
        earlier[0] + later_pair[0],
        jnp.exp(later_pair[0])[:, None, None] * earlier[1] + later_pair[1],
    )


def select_rows(routes, expert_ids, capacity, source):
    chosen = jnp.any(routes[None, :, :] == expert_ids[:, None, None], axis=2).astype(jnp.int32)
    position = jnp.cumsum(chosen, axis=1) - 1
    slot_ids = jnp.arange(capacity, dtype=jnp.int32)
    selector = (
        (chosen[:, None, :] == 1) & (position[:, None, :] == slot_ids[None, :, None])
    ).astype(jnp.bfloat16)
    return jnp.einsum("nct,tf->ncf", selector, source, preferred_element_type=jnp.float32).astype(
        jnp.bfloat16
    )


def shards(queries, keys, values, log_decay, state_in, norm_gain, routes, w_gate, w_up):
    length = queries.shape[0]
    features = queries.shape[1]
    local_heads = state_in.shape[0]
    head_dim = state_in.shape[1]
    scaling = 1.0 / math.sqrt(head_dim)
    query_blk = queries.reshape(length, local_heads, head_dim)
    key_blk = keys.reshape(length, local_heads, head_dim)
    value_blk = values.reshape(length, local_heads, head_dim)
    cumlog = jnp.cumsum(log_decay, axis=1)
    block_log = cumlog[:, -1]
    causal = jnp.arange(length)[:, None] >= jnp.arange(length)[None, :]
    scores = (
        jnp.einsum("ihd,jhd->hij", query_blk, key_blk, preferred_element_type=jnp.float32) * scaling
    )
    gap_log = cumlog[:, :, None] - cumlog[:, None, :]
    weights = jnp.where(causal[None], jnp.exp(jnp.where(causal[None], gap_log, 0.0)), 0.0)
    decayed = (scores * weights).astype(jnp.bfloat16)
    inside = jnp.einsum("hij,jhd->ihd", decayed, value_blk, preferred_element_type=jnp.float32)
    key_weighted = key_blk.astype(jnp.float32) * jnp.exp(block_log[:, None] - cumlog).T[:, :, None]
    block_state = jnp.einsum(
        "jhd,jhe->hde", key_weighted, value_blk.astype(jnp.float32), precision=lax.Precision.HIGHEST
    )
    before_log, before_state = prefix(
        (block_log, block_state),
        "seq",
        compose,
        (jnp.zeros_like(block_log), jnp.zeros_like(block_state)),
    )
    entering = jnp.exp(before_log)[:, None, None] * state_in + before_state
    carried_in = jnp.einsum(
        "ihd,hde->ihe",
        query_blk.astype(jnp.float32) * scaling,
        entering,
        precision=lax.Precision.HIGHEST,
    )
    carried_in = carried_in * jnp.exp(cumlog).T[:, :, None]
    attended = (inside + carried_in).astype(jnp.bfloat16).reshape(length, features)
    chain_log = lax.psum(block_log, "seq")
    later_log = chain_log - before_log - block_log
    weighted = jnp.exp(later_log)[:, None, None] * block_state
    reduced = lax.psum_scatter(weighted, "seq", scatter_dimension=1, tiled=True)
    row_count = reduced.shape[1]
    carried_rows = lax.dynamic_slice_in_dim(
        state_in, lax.axis_index("seq") * row_count, row_count, 1
    )
    state_out = reduced + jnp.exp(chain_log)[:, None, None] * carried_rows
    local_experts = w_gate.shape[0]
    gathered = lax.all_gather(attended, "exp", axis=1, tiled=True)
    expert_ids = lax.axis_index("exp") * local_experts + jnp.arange(local_experts, dtype=jnp.int32)
    row_set = select_rows(routes, expert_ids, CAP, gathered)
    row_wide = row_set.astype(jnp.float32)
    normed = (
        row_wide
        * lax.rsqrt(jnp.mean(row_wide * row_wide, axis=2, keepdims=True) + epsilon)
        * norm_gain
    ).astype(jnp.bfloat16)
    block_part = lax.all_gather(normed, "seq", axis=1, tiled=True)
    gate_act = jnp.einsum("efd,end->efn", w_gate, block_part, preferred_element_type=jnp.float32)
    up_act = jnp.einsum("efd,end->efn", w_up, block_part, preferred_element_type=jnp.float32)
    expert_hidden = (jax.nn.silu(gate_act) * up_act).astype(jnp.bfloat16)
    return (expert_hidden, state_out)


def solution(mesh):
    placed = (
        P("seq", "exp"),
        P("seq", "exp"),
        P("seq", "exp"),
        P("exp", "seq"),
        P("exp", None, None),
        P(),
        P("seq", None),
        P("exp", "seq", None),
        P("exp", "seq", None),
    )
    return jax.shard_map(
        shards,
        mesh=mesh,
        in_specs=placed,
        out_specs=(P("exp", "seq", None), P("exp", "seq", None)),
        check_vma=False,
    )
```

profile of v0, /device:TPU:1, one launch (start us, length us, event | category | flops | bytes accessed | tf_op | source)
XLA Modules:
  0.0 845.0 jit_solution(10170178238828046064)
XLA Ops:
  7.2 0.0 copy-start
  7.2 0.0 all-gather.7.cloned.1.call-start
  7.2 1.0 reduce_window_sum.18
  8.2 0.2 slice_reduce_fusion
  8.4 0.1 exponential_bitcast_fusion
  8.5 0.1 copy.27
  8.6 1.0 reshape.163
  9.6 0.1 convert_multiply_fusion.1
  9.8 2.2 fusion.16
  12.0 0.0 all-gather.7.cloned.1.call-update
  12.0 0.0 all-reduce.5.cloned.1.call-start
  12.0 1.4 fusion.46
  14.1 0.2 dynamic-update-slice
  14.3 123.5 %all-reduce.2 = (f32[384]{0:T(512)S(1)}, f32[6]{0:T(128)S(1)}) all-reduce(f32[384]{0:T(512)S(1)} %dynamic-update-slice, f32[6]{0:T(128)S(1)} %slice_reduce_fusion), channel_id=2, replica_groups=mesh['seq'=64,'exp'=8] {'seq'}, use_global_device_ids=true, to_apply=%add | all-reduce | flops 390 | bytes 3120
  137.8 0.1 reshape.170
  137.9 0.7 compare_reduce_fusion
  138.6 0.1 copy.23
  138.7 0.1 reduce-window.7
  138.8 1.0 reshape.162
  139.9 0.1 add_reduce_fusion
  140.0 1.3 convolution_bitcast_fusion.3
  141.3 120.3 %all-gather.7.cloned.1.call-done = f32[384,128,128]{2,1,0:T(8,128)} async-done(((f32[6,128,128]{2,1,0:T(8,128)}), f32[384,128,128]{2,1,0:T(8,128)}) %all-gather.7.cloned.1.call-update) | async-done | bytes 25165840 | tf_op jit(solution)/shard_map/all_gather | solution.py:13
  261.7 1.6 fusion.11
  263.3 1.9 broadcast_multiply_fusion
  265.2 0.0 all-reduce.5.cloned.1.call-update
  265.2 0.0 all-gather.9.cloned.1.call-start
  265.3 14.6 %all_gather.18 = bf16[64,6144]{1,0:T(8,128)(2,1)S(1)} all-gather(bf16[64,768]{1,0:T(8,128)(2,1)S(1)} %bitcast.90), channel_id=1, replica_groups=mesh['seq'=64,'exp'=8] {'exp'}, dimensions={1}, use_global_device_ids=true | all-gather | bytes 884736 | tf_op jit(solution)/shard_map/all_gather | solution.py:91
  279.9 0.3 multiply_reduce_fusion
  280.3 1.6 fusion.14
  281.9 0.0 all-gather.9.cloned.1.call-update
  282.5 301.2 %all-reduce.5.cloned.1.call-done = f32[6,128,128]{2,1,0:T(8,128)} async-done(((f32[6,128,128]{2,1,0:T(8,128)}), f32[6,128,128]{2,1,0:T(8,128)}) %all-reduce.5.cloned.1.call-update) | async-done | bytes 393232
  583.8 1.4 dynamic-slice_add_fusion
  585.2 212.3 %all-gather.9.cloned.1.call-done = bf16[64,20,6144]{2,1,0:T(8,128)(2,1)} async-done(((bf16[1,20,6144]{2,1,0:T(8,128)(2,1)}), bf16[64,20,6144]{2,1,0:T(8,128)(2,1)}) %all-gather.9.cloned.1.call-update) | async-done | bytes 15728656 | tf_op jit(solution)/shard_map/all_gather | solution.py:100
  797.5 23.9 %reshape.178 = bf16[1280,6144]{1,0:T(8,128)(2,1)} reshape(bf16[64,20,6144]{2,1,0:T(8,128)(2,1)} %all-gather.9.cloned.1.call-done) | data formatting | bytes 31457280
  821.4 0.0 copy-done
  821.4 0.0 copy-start.1
  821.4 0.0 copy-start.2
  821.4 11.0 %convolution_bitcast_fusion.1 = f32[144,1280]{1,0:T(8,128)S(1)} fusion(bf16[1280,6144]{1,0:T(8,128)(2,1)} %reshape.178, bf16[1,144,6144]{2,1,0:T(8,128)(2,1)S(1)} %copy-done), kind=kOutput, calls=%fused_computation.8 | convolution fusion | flops 2264924160 | bytes 18235392 | tf_op jit(solution)/shard_map/efd,end->efn/dot_general | solution.py:101
  832.4 0.0 copy-done.1
  832.4 0.0 copy-done.2
  832.4 6.1 fusion.3
  (10 shorter events, 0.1 us)
Async XLA Ops:
  7.2 814.2 %copy-start = (bf16[1,144,6144]{2,1,0:T(8,128)(2,1)S(1)}, bf16[1,144,6144]{2,1,0:T(8,128)(2,1)}, u32[]{:S(2)}) copy-start(bf16[1,144,6144]{2,1,0:T(8,128)(2,1)} %param.18) | copy-start | bytes 5308420
  7.2 254.5 %all-gather.7.cloned.1.call-start = ((), (), s32[]{:S(2)}) async-start(), calls=%async_computation | async-start | bytes 25559040 | tf_op jit(solution)/shard_map/all_gather | solution.py:13
  12.0 571.8 %all-reduce.5.cloned.1.call-start = ((), (), s32[]{:S(2)}) async-start(), calls=%async_computation.2 | async-start | bytes 786432
  265.2 532.3 %all-gather.9.cloned.1.call-start = ((), (), s32[]{:S(2)}) async-start(), calls=%async_computation.1 | async-start | bytes 19169280 | tf_op jit(solution)/shard_map/all_gather | solution.py:100
  821.4 11.0 %copy-start.1 = (bf16[1280,6144]{1,0:T(8,128)(2,1)S(1)}, bf16[1280,6144]{1,0:T(8,128)(2,1)}, u32[]{:S(2)}) copy-start(bf16[1280,6144]{1,0:T(8,128)(2,1)} %reshape.178) | copy-start | bytes 47185924
  821.4 11.0 %copy-start.2 = (bf16[1,144,6144]{2,1,0:T(8,128)(2,1)S(1)}, bf16[1,144,6144]{2,1,0:T(8,128)(2,1)}, u32[]{:S(2)}) copy-start(bf16[1,144,6144]{2,1,0:T(8,128)(2,1)} %param.19) | copy-start | bytes 5308420
Sparse Core Ops, SparseCore 0:
  12.1 249.5 all-gather.6
  265.3 318.3 all-reduce.4
  587.3 210.1 all-gather.8
where the time goes:
time: 849 us; the launch traced here: 845 us
  waiting for transfers between devices  634 us (75%)
  blocking collectives  138 us (16%)
  local copies, waits for them, and re-layouts  28.1 us (3%)
  matrix products  22.5 us (3%)
  between operations  15.2 us (2%)
    unnamed x4, waiting for transfers between devices  301 us
    all_gather x1, waiting for transfers between devices, shards(): block_part = lax.all_gather(normed, 'seq', axis=1, tiled=True)  212 us
    unnamed x1, blocking collectives  123 us
    all_gather x1, waiting for transfers between devices, prefix(): gathered = jax.tree.map(lambda a: lax.all_gather(a, axis), part)  120 us
    unnamed x10, local copies, waits for them, and re-layouts  25.5 us
  transfers between devices with their start and end apart: 3, of which 3 were waited for; matrix products, arithmetic and copies ran while one was open for 1% of the time, Pallas kernels for 0%

commit v1 on v0

--- a/solution.py
+++ b/solution.py
@@ -97,7 +97,9 @@
         * lax.rsqrt(jnp.mean(row_wide * row_wide, axis=2, keepdims=True) + epsilon)
         * norm_gain
     ).astype(jnp.bfloat16)
-    block_part = lax.all_gather(normed, "seq", axis=1, tiled=True)
+    block_part = jnp.concatenate(
+        lax.all_to_all(jnp.stack([normed] * lax.axis_size("seq")), "seq", 0, 0), axis=1
+    )
     gate_act = jnp.einsum("efd,end->efn", w_gate, block_part, preferred_element_type=jnp.float32)
     up_act = jnp.einsum("efd,end->efn", w_up, block_part, preferred_element_type=jnp.float32)
     expert_hidden = (jax.nn.silu(gate_act) * up_act).astype(jnp.bfloat16)

time: 849 us -> 1250 us (1.47)
  waiting for transfers between devices: 634 us -> 944 us
  starting transfers between devices: 0.12 us -> 78.1 us
    unnamed x4 -> x3, waiting for transfers between devices: 301 us -> 587 us
    all_to_all x0 -> x1, waiting for transfers between devices: none -> 237 us  [shards(): lax.all_to_all(jnp.stack([normed] * lax.axis_size('seq')), 'seq', 0, 0)]
    all_gather x1 -> x0, waiting for transfers between devices: 212 us -> none  [shards(): block_part = lax.all_gather(normed, 'seq', axis=1, tiled=True)]
    all_to_all x0 -> x1, starting transfers between devices: none -> 77.9 us  [shards(): lax.all_to_all(jnp.stack([normed] * lax.axis_size('seq')), 'seq', 0, 0)]
    another operation x1 -> x3, local copies, waits for them, and re-layouts: 0.01 us -> 30.7 us
    unnamed x10 -> x11, local copies, waits for them, and re-layouts: 25.5 us -> 1.62 us
where the time goes in v1:
time: 1250 us; the launch traced here: 1240 us
  waiting for transfers between devices  944 us (76%)
  blocking collectives  138 us (11%)
  starting transfers between devices  78.1 us (6%)
  local copies, waits for them, and re-layouts  34.9 us (3%)
  matrix products  22.4 us (2%)
  between operations  15.4 us (1%)
    unnamed x3, waiting for transfers between devices  587 us
    all_to_all x1, waiting for transfers between devices, shards(): lax.all_to_all(jnp.stack([normed] * lax.axis_size('seq')), 'seq', 0, 0)  237 us
    unnamed x1, blocking collectives  123 us
    all_gather x1, waiting for transfers between devices, prefix(): gathered = jax.tree.map(lambda a: lax.all_gather(a, axis), part)  120 us
    all_to_all x1, starting transfers between devices, shards(): lax.all_to_all(jnp.stack([normed] * lax.axis_size('seq')), 'seq', 0, 0)  77.9 us
  transfers between devices with their start and end apart: 3, of which 3 were waited for; matrix products, arithmetic and copies ran while one was open for 1% of the time, Pallas kernels for 0%

profile of v1, /device:TPU:1, one launch (start us, length us, event | category | flops | bytes accessed | tf_op | source)
XLA Modules:
  0.0 1238.6 jit_solution(6160103532154334917)
XLA Ops:
  7.2 0.0 copy-start
  7.2 0.0 all-gather.4.cloned.1.call-start
  7.2 1.0 reduce_window_sum.18
  8.2 0.2 slice_reduce_fusion
  8.4 0.1 exponential_bitcast_fusion
  8.5 0.1 copy.27
  8.6 1.0 reshape.169
  9.6 0.1 convert_multiply_fusion.1
  9.8 2.1 fusion.15
  11.9 0.0 all-gather.4.cloned.1.call-update
  12.0 1.4 fusion.45
  13.9 0.2 dynamic-update-slice
  14.1 123.5 %all-reduce.2 = (f32[384]{0:T(512)S(1)}, f32[6]{0:T(128)S(1)}) all-reduce(f32[384]{0:T(512)S(1)} %dynamic-update-slice, f32[6]{0:T(128)S(1)} %slice_reduce_fusion), channel_id=2, replica_groups=mesh['seq'=64,'exp'=8] {'seq'}, use_global_device_ids=true, to_apply=%add | all-reduce | flops 390 | bytes 3120
  137.6 0.1 reshape.176
  137.7 0.7 compare_reduce_fusion
  138.4 0.1 copy.23
  138.5 0.1 reduce-window.7
  138.6 1.0 reshape.168
  139.7 0.1 add_reduce_fusion
  139.8 1.3 convolution_bitcast_fusion.3
  141.1 120.5 %all-gather.4.cloned.1.call-done = f32[384,128,128]{2,1,0:T(8,128)} async-done(((f32[6,128,128]{2,1,0:T(8,128)}), f32[384,128,128]{2,1,0:T(8,128)}) %all-gather.4.cloned.1.call-update) | async-done | bytes 25165840 | tf_op jit(solution)/shard_map/all_gather | solution.py:13
  261.7 1.6 fusion.11
  263.3 14.6 %all_gather.15 = bf16[64,6144]{1,0:T(8,128)(2,1)S(1)} all-gather(bf16[64,768]{1,0:T(8,128)(2,1)S(1)} %bitcast.88), channel_id=1, replica_groups=mesh['seq'=64,'exp'=8] {'exp'}, dimensions={1}, use_global_device_ids=true | all-gather | bytes 884736 | tf_op jit(solution)/shard_map/all_gather | solution.py:91
  277.9 0.3 multiply_reduce_fusion
  278.3 0.9 multiply_convert_fusion
  279.1 6.8 stack.2
  285.9 0.0 copy-start.2
  285.9 77.9 %all-to-all-start = ((bf16[64,1,20,6144]{3,2,1,0:T(8,128)(2,1)}), bf16[64,1,20,6144]{3,2,1,0:T(8,128)(2,1)}, u32[]{:S(2)}, u32[]{:S(2)}) async-start(bf16[64,1,20,6144]{3,2,1,0:T(8,128)(2,1)} %stack.2), calls=%async_computation | async-start | bytes 37748736 | tf_op jit(solution)/shard_map/all_to_all | solution.py:101
  363.8 0.2 all-reduce.5.cloned.1.call-start
  364.0 0.0 copy-done.2
  364.0 0.8 broadcast_multiply_fusion
  364.9 0.0 all-reduce.5.cloned.1.call-update
  365.5 586.6 %all-reduce.5.cloned.1.call-done = f32[6,128,128]{2,1,0:T(8,128)} async-done(((f32[6,128,128]{2,1,0:T(8,128)}), f32[6,128,128]{2,1,0:T(8,128)}) %all-reduce.5.cloned.1.call-update) | async-done | bytes 393232
  952.2 1.4 dynamic-slice_add_fusion
  953.6 237.2 %all-to-all-done = bf16[64,1,20,6144]{3,2,1,0:T(8,128)(2,1)} async-done(((bf16[64,1,20,6144]{3,2,1,0:T(8,128)(2,1)}), bf16[64,1,20,6144]{3,2,1,0:T(8,128)(2,1)}, u32[]{:S(2)}, u32[]{:S(2)}) %all-to-all-start) | async-done | bytes 15728672 | tf_op jit(solution)/shard_map/all_to_all | solution.py:101
  1190.8 23.9 %reshape.172 = bf16[1280,6144]{1,0:T(8,128)(2,1)} reshape(bf16[64,1,20,6144]{3,2,1,0:T(8,128)(2,1)} %all-to-all-done) | data formatting | bytes 31457280 | tf_op jit(solution)/shard_map/reshape.17
  1214.7 0.0 copy-done
  1214.7 0.0 copy-start.1
  1214.7 0.0 copy-start.3
  1214.7 11.0 convolution_bitcast_fusion.1
  1225.7 0.0 copy-done.1
  1225.7 0.0 copy-done.3
  1225.7 6.1 fusion.3
  (10 shorter events, 0.1 us)
Async XLA Ops:
  7.2 1207.5 %copy-start = (bf16[1,144,6144]{2,1,0:T(8,128)(2,1)S(1)}, bf16[1,144,6144]{2,1,0:T(8,128)(2,1)}, u32[]{:S(2)}) copy-start(bf16[1,144,6144]{2,1,0:T(8,128)(2,1)} %param.18) | copy-start | bytes 5308420
  7.2 254.4 %all-gather.4.cloned.1.call-start = ((), (), s32[]{:S(2)}) async-start(), calls=%async_computation.1 | async-start | bytes 25559040 | tf_op jit(solution)/shard_map/all_gather | solution.py:13
  285.9 78.1 %copy-start.2 = (f32[6,128,128]{2,1,0:T(8,128)S(1)}, f32[6,128,128]{2,1,0:T(8,128)}, u32[]{:S(2)}) copy-start(f32[6,128,128]{2,1,0:T(8,128)} %fusion.15) | copy-start | bytes 1179652
  285.9 904.9 %all-to-all-start = ((bf16[64,1,20,6144]{3,2,1,0:T(8,128)(2,1)}), bf16[64,1,20,6144]{3,2,1,0:T(8,128)(2,1)}, u32[]{:S(2)}, u32[]{:S(2)}) async-start(bf16[64,1,20,6144]{3,2,1,0:T(8,128)(2,1)} %stack.2), calls=%async_computation | async-start | bytes 37748736 | tf_op jit(solution)/shard_map/all_to_all | solution.py:101
  363.8 588.4 %all-reduce.5.cloned.1.call-start = ((), (), s32[]{:S(2)}) async-start(), calls=%async_computation.2 | async-start | bytes 786432
  1214.7 11.0 copy-start.1
  1214.7 11.0 copy-start.3
Sparse Core Ops, SparseCore 0:
  12.1 249.4 all-gather.3
  368.1 584.0 all-reduce.4
